TPU v7x, 256 devices: a whole 4x4x8 slice. The times are simulated.
256 devices in a mesh: dp: 4 (over z_hi), expert: 64 (over z_lo, y, x, core).
Axes of the slice: x: 4, y: 4, z: 8 (z_hi: 4, z_lo: 2; z = z_hi * 2 + z_lo), core: 2. Of those that a mesh axis runs over, the one named last changes fastest.
Arguments:
- grad_out: bfloat16 [40960, 3584], P(('dp', 'expert')), may hold values from -1.5 to 1.5
- routes: int32 [40960, 2], P(('dp', 'expert')), may hold values from 0 to 63, all different within a row; in each aligned block of 160 rows (0 to 159, 160 to 319, ...) at most 10 rows name the same one
- route_weight: bfloat16 [40960, 2], P(('dp', 'expert')), may hold values from 0.099609375 to 1
- hidden_saved: bfloat16 [64, 4, 64, 10, 1024], P('expert', 'dp'), may hold values from -6 to 6
- down_weight: bfloat16 [64, 1024, 3584], P('expert', 'dp'), may hold values from -0.1875 to 0.1875
Outputs:
- down_grad: float32 [64, 1024, 3584], P('expert', 'dp')
- hidden_grad: bfloat16 [64, 4, 64, 10, 1024], P('expert', 'dp')
- prob_grad: float32 [40960, 2], P(('dp', 'expert'))
Inputs may be any that keep to these rules, and one draw needn't show every extreme that they name: `routes`: each row names 2 different experts; among the rows of one device no expert is named by more than 10 rows, a bound that some block reaches; every expert is named somewhere.
All inputs are finite; a program needn't handle non-finite values.
Results may differ from a plain program's by a relative error of at most 0.014.
Values may be sent and summed in bfloat16 or wider, within the bound.
A program may use at most 128 MiB of HBM per device.

v0:
```python
import jax
import jax.numpy as jnp
from jax import lax
from jax.sharding import PartitionSpec as P


def per_device(grad_out, routes, route_weight, hidden_saved, down_weight):
    token_count, model_width = grad_out.shape
    route_count = routes.shape[1]
    expert_count = lax.axis_size("expert")
    capacity = hidden_saved.shape[3]
    hidden_width = hidden_saved.shape[4]
    slot_total = expert_count * capacity
    flat_routes = routes.reshape(-1)
    member = (flat_routes[:, None] == jnp.arange(expert_count, dtype=jnp.int32)[None, :]).astype(
        jnp.int32
    )
    earlier = jnp.cumsum(member, axis=0) - member
    slot_index = jnp.sum(earlier * member, axis=1)
    destination = flat_routes * capacity + slot_index
    token_index = jnp.arange(token_count * route_count, dtype=jnp.int32) // route_count
    send_rows = (
        jnp.zeros((slot_total, model_width), jnp.bfloat16)
        .at[destination]
        .set(grad_out[token_index])
    )
    send_weights = (
        jnp.zeros((slot_total,), jnp.bfloat16).at[destination].set(route_weight.reshape(-1))
    )
    got_rows, got_weights = (
        lax.all_to_all(
            send_rows.reshape(expert_count, capacity, model_width),
            "expert",
            split_axis=0,
            concat_axis=0,
            tiled=True,
        ),
        lax.all_to_all(
            send_weights.reshape(expert_count, capacity),
            "expert",
            split_axis=0,
            concat_axis=0,
            tiled=True,
        ),
    )
    sent_rows = got_rows.reshape(slot_total, model_width)
    slot_weights = got_weights.reshape(slot_total, 1).astype(jnp.float32)
    hidden = hidden_saved.reshape(slot_total, hidden_width)
    scaled = (slot_weights * sent_rows.astype(jnp.float32)).astype(jnp.bfloat16)
    weight_rows = down_weight.reshape(down_weight.shape[1], model_width)
    share = weight_rows.shape[0]
    contract_last = (((1,), (1,)), ((), ()))
    contract_first = (((0,), (0,)), ((), ()))
    piece = lax.all_gather(weight_rows, "dp", axis=0, tiled=True)
    columns = hidden
    output_sum = jnp.dot(columns, piece, preferred_element_type=jnp.float32)
    product = lax.dot_general(scaled, piece, contract_last, preferred_element_type=jnp.float32)
    slot_prob = jnp.sum(sent_rows.astype(jnp.float32) * output_sum, axis=1)
    hidden_grad = product.astype(jnp.bfloat16)
    columns = hidden
    down_grad = lax.psum_scatter(
        lax.dot_general(columns, scaled, contract_first, preferred_element_type=jnp.float32).astype(
            jnp.bfloat16
        ),
        "dp",
        scatter_dimension=0,
        tiled=True,
    ).astype(jnp.float32)
    returned = lax.all_to_all(
        slot_prob.reshape(expert_count, capacity), "expert", split_axis=0, concat_axis=0, tiled=True
    )
    prob_grad = returned.reshape(-1)[destination].reshape(token_count, route_count)
    return (
        down_grad.reshape(1, share, model_width),
        hidden_grad.reshape(hidden_saved.shape),
        prob_grad,
    )


def solution(mesh):
    placed = (
        P(("dp", "expert"), None),
        P(("dp", "expert"), None),
        P(("dp", "expert"), None),
        P("expert", "dp", None, None, None),
        P("expert", "dp", None),
    )
    return jax.shard_map(
        per_device,
        mesh=mesh,
        in_specs=placed,
        out_specs=(
            P("expert", "dp", None),
            P("expert", "dp", None, None, None),
            P(("dp", "expert"), None),
        ),
        check_vma=False,
    )
```

profile of v0, /device:TPU:1, one launch (start us, length us, event | category | flops | bytes accessed | tf_op | source)
XLA Modules:
  0.0 435.2 jit_solution(12955747562059871387)
XLA Ops:
  7.2 0.9 copy.20
  8.1 0.7 broadcast_multiply_fusion
  8.9 0.9 reduce-window.6
  9.8 0.2 slice_reduce_fusion
  10.5 0.8 copy.23
  11.5 2.6 scatter_custom_fusion
  14.1 0.8 all_to_all.20
  14.9 10.4 %all-to-all-start = ((bf16[64,1,10]{2,1,0:T(2,128)(2,1)}), bf16[64,1,10]{2,1,0:T(2,128)(2,1)S(1)}, u32[]{:S(2)}, u32[]{:S(2)}) async-start(bf16[64,1,10]{2,1,0:T(2,128)(2,1)} %all_to_all.20), calls=%async_computation | async-start | bytes 65536 | tf_op jit(solution)/shard_map/all_to_all | solution.py:38
  25.3 13.2 %scatter_custom_fusion.1 = bf16[640,3584]{1,0:T(8,128)(2,1)} fusion(s32[320]{0:T(512)S(1)} %fusion.16, bf16[160,3584]{1,0:T(8,128)(2,1)S(1)} %copy-done, s32[1024]{0:T(1024)S(1)} %pad_clamp_fusion.1, bf16[]{:T(256)} %constant.26.clone.1), kind=kCustom, calls=%fused_computation.14 | custom fusion | bytes 4587522 | tf_op jit(solution)/shard_map/scatter | solution.py:25
  38.5 7.7 %reshape.152 = bf16[64,10,3584]{2,1,0:T(8,128)(2,1)} reshape(bf16[640,3584]{1,0:T(8,128)(2,1)} %scatter_custom_fusion.1) | data formatting | bytes 9175040 | tf_op jit(solution)/shard_map/reshape | solution.py:32
  46.2 9.1 %all-to-all-start.1 = ((bf16[64,10,3584]{2,1,0:T(8,128)(2,1)}), bf16[64,10,3584]{2,1,0:T(8,128)(2,1)}, u32[]{:S(2)}, u32[]{:S(2)}) async-start(bf16[64,10,3584]{2,1,0:T(8,128)(2,1)} %reshape.152), calls=%async_computation.1 | async-start | bytes 14680064 | tf_op jit(solution)/shard_map/all_to_all | solution.py:31
  55.3 0.7 all-gather.3.cloned.1.call-update
  56.0 2.1 copy.25
  58.2 1.3 reshape.153
  59.5 197.4 %all-to-all-done.1 = bf16[64,10,3584]{2,1,0:T(8,128)(2,1)} async-done(((bf16[64,10,3584]{2,1,0:T(8,128)(2,1)}), bf16[64,10,3584]{2,1,0:T(8,128)(2,1)}, u32[]{:S(2)}, u32[]{:S(2)}) %all-to-all-start.1) | async-done | bytes 4587552 | tf_op jit(solution)/shard_map/all_to_all | solution.py:31
  256.9 8.5 %multiply_convert_fusion = bf16[64,10,3584]{2,1,0:T(8,128)(2,1)} fusion(f32[64,10]{1,0:T(8,128)S(1)} %bitcast.32, bf16[64,10,3584]{2,1,0:T(8,128)(2,1)} %all-to-all-done.1), kind=kLoop, calls=%fused_computation.4 | loop fusion | flops 6881280 | bytes 9177600 | tf_op jit(solution)/shard_map/convert_element_type | solution.py:49
  265.5 8.0 %convert_element_type.54 = bf16[640,3584]{1,0:T(8,128)(2,1)} reshape(bf16[64,10,3584]{2,1,0:T(8,128)(2,1)} %multiply_convert_fusion) | data formatting | bytes 9175040 | tf_op jit(solution)/shard_map/convert_element_type | solution.py:49
  273.5 10.3 %fusion.4 = bf16[1024,3584]{0,1:T(8,128)(2,1)} fusion(bf16[640,3584]{1,0:T(8,128)(2,1)} %convert_element_type.54, bf16[640,1024]{1,0:T(8,128)(2,1)S(1)} %copy-done.2), kind=kOutput, calls=%fused_computation.12 | convolution fusion | flops 4701290496 | bytes 13238272 | tf_op jit(solution)/shard_map/dot_general | solution.py:62
  284.1 9.1 %reshape.165 = f32[640,3584]{1,0:T(8,128)} reshape(bf16[64,10,3584]{2,1,0:T(8,128)(2,1)} %all-to-all-done.1) | data formatting | bytes 13762560 | tf_op jit(solution)/shard_map/convert_element_type | solution.py:49
  293.2 12.0 %multiply_reduce_fusion = f32[640]{0:T(1024)S(1)} fusion(f32[640,3584]{1,0:T(8,128)} %reshape.165, bf16[640,1024]{1,0:T(8,128)(2,1)S(1)} %copy-done.2, bf16[1,1024,3584]{2,1,0:T(8,128)(2,1)} %all-gather.3.cloned.1.call-done), kind=kOutput, calls=%fused_computation.5 | convolution fusion | flops 4702207488 | bytes 17828352 | tf_op jit(solution)/shard_map/dot_general | solution.py:56
  305.2 0.8 all_to_all.18
  306.0 8.5 %all-to-all-start.2 = ((f32[64,1,10]{2,1,0:T(1,128)}), f32[64,1,10]{2,1,0:T(1,128)S(1)}, u32[]{:S(2)}, u32[]{:S(2)}) async-start(f32[64,1,10]{2,1,0:T(1,128)} %bitcast.5), calls=%async_computation.3 | async-start | bytes 65536 | tf_op jit(solution)/shard_map/all_to_all | solution.py:69
  314.4 11.7 %fusion.11 = bf16[640,1024]{1,0:T(8,128)(2,1)} fusion(bf16[1,1024,3584]{2,1,0:T(8,128)(2,1)} %all-gather.3.cloned.1.call-done, f32[640,3584]{1,0:T(8,128)} %reshape.165, f32[640]{0:T(1024)S(1)} %reshape.164), kind=kOutput, calls=%fused_computation.18 | convolution fusion | flops 4702863360 | bytes 17828352 | tf_op jit(solution)/shard_map/dot_general | solution.py:57
  326.1 2.4 reshape.157
  328.5 1.8 copy.28
  330.3 0.5 broadcast.126
  330.8 0.7 reduce.13
  331.7 1.7 gather_fusion
  333.5 0.7 copy.29
  334.1 85.5 %reduce-scatter.2.cloned.1.call-done = bf16[256,3584]{0,1:T(8,128)(2,1)} async-done(((bf16[1024,3584]{0,1:T(8,128)(2,1)}), bf16[256,3584]{0,1:T(8,128)(2,1)}) %reduce-scatter.2.cloned.1.call-update) | async-done | bytes 1835024 | tf_op jit(solution)/shard_map/reduce_scatter | solution.py:61
  419.6 3.7 bitcast_convert_fusion
  423.3 5.1 %copy.27 = f32[1,256,3584]{2,1,0:T(8,128)} copy(f32[1,256,3584]{1,2,0:T(8,128)} %bitcast_convert_fusion) | data formatting | bytes 7340032
  (30 shorter events, 1.5 us)
Async XLA Ops:
  7.2 18.1 %copy-start = (bf16[160,3584]{1,0:T(8,128)(2,1)S(1)}, bf16[160,3584]{1,0:T(8,128)(2,1)}, u32[]{:S(2)}) copy-start(bf16[160,3584]{1,0:T(8,128)(2,1)} %param.5) | copy-start | bytes 3440644
  14.9 31.3 %all-to-all-start = ((bf16[64,1,10]{2,1,0:T(2,128)(2,1)}), bf16[64,1,10]{2,1,0:T(2,128)(2,1)S(1)}, u32[]{:S(2)}, u32[]{:S(2)}) async-start(bf16[64,1,10]{2,1,0:T(2,128)(2,1)} %all_to_all.20), calls=%async_computation | async-start | bytes 65536 | tf_op jit(solution)/shard_map/all_to_all | solution.py:38
  46.2 210.7 %all-to-all-start.1 = ((bf16[64,10,3584]{2,1,0:T(8,128)(2,1)}), bf16[64,10,3584]{2,1,0:T(8,128)(2,1)}, u32[]{:S(2)}, u32[]{:S(2)}) async-start(bf16[64,10,3584]{2,1,0:T(8,128)(2,1)} %reshape.152), calls=%async_computation.1 | async-start | bytes 14680064 | tf_op jit(solution)/shard_map/all_to_all | solution.py:31
  55.3 237.9 %all-gather.3.cloned.1.call-start = ((), (), s32[]{:S(2)}) async-start(), calls=%async_computation.5 | async-start | bytes 9175040 | tf_op jit(solution)/shard_map/all_gather | solution.py:54
  56.0 363.6 %reduce-scatter.2.cloned.1.call-start = ((), (), s32[]{:S(2)}) async-start(), calls=%async_computation.4 | async-start | bytes 9175040 | tf_op jit(solution)/shard_map/reduce_scatter | solution.py:61
  265.5 8.1 %copy-start.2 = (bf16[640,1024]{1,0:T(8,128)(2,1)S(1)}, bf16[640,1024]{1,0:T(8,128)(2,1)}, u32[]{:S(2)}) copy-start(bf16[640,1024]{1,0:T(8,128)(2,1)} %reshape.153) | copy-start | bytes 3932164
  306.0 24.3 %all-to-all-start.2 = ((f32[64,1,10]{2,1,0:T(1,128)}), f32[64,1,10]{2,1,0:T(1,128)S(1)}, u32[]{:S(2)}, u32[]{:S(2)}) async-start(f32[64,1,10]{2,1,0:T(1,128)} %bitcast.5), calls=%async_computation.3 | async-start | bytes 65536 | tf_op jit(solution)/shard_map/all_to_all | solution.py:69
  419.6 8.8 %copy-start.1 = (bf16[160,3584]{1,0:T(8,128)(2,1)S(1)}, bf16[160,3584]{1,0:T(8,128)(2,1)}, u32[]{:S(2)}) copy-start(bf16[160,3584]{1,0:T(8,128)(2,1)} %param.5) | copy-start | bytes 3440644
Sparse Core Ops, SparseCore 0:
  57.9 198.5 all-gather.2
  284.0 135.5 reduce-scatter.1
where the time goes:
time: 437 us; the launch traced here: 435 us
  waiting for transfers between devices  284 us (65%)
  local copies, waits for them, and re-layouts  60.5 us (14%)
  matrix products  34 us (8%)
  starting transfers between devices  28 us (6%)
  other arithmetic  14.9 us (3%)
  between operations  14.2 us (3%)
    all_to_all x1, waiting for transfers between devices, per_device(): lax.all_to_all(send_rows.reshape(expert_count, capacity, model_width), 'e...  197 us
    reduce_scatter x1, waiting for transfers between devices, per_device(): lax.psum_scatter(lax.dot_general(columns, scaled, contract_first, preferr...  85.5 us
    convert_element_type x2, local copies, waits for them, and re-layouts, per_device(): scaled = (slot_weights * sent_rows.astype(jnp.float32)).astype(jnp.bfloat16)  17.1 us
    scatter x1, local copies, waits for them, and re-layouts, per_device(): send_rows = jnp.zeros((slot_total, model_width), jnp.bfloat16).at[destina...  13.2 us
    dot_general x1, matrix products, per_device(): output_sum = jnp.dot(columns, piece, preferred_element_type=jnp.float32)  12 us
    dot_general x1, matrix products, per_device(): lax.dot_general(scaled, piece, contract_last, preferred_element_type=jnp....  11.7 us
    unnamed x12, local copies, waits for them, and re-layouts  11.4 us
    all_to_all x1, starting transfers between devices, per_device(): lax.all_to_all(send_weights.reshape(expert_count, capacity), 'expert', sp...  10.4 us
  transfers between devices with their start and end apart: 5, of which 2 were waited for; matrix products, arithmetic and copies ran while one was open for 21% of the time, Pallas kernels for 0%

commit v1 on v0

v1 whole, which is shorter than its diff:
```python
import functools

import jax
import jax.numpy as jnp
from jax import lax
from jax.experimental import pallas as pl
from jax.experimental.pallas import tpu as pltpu
from jax.sharding import PartitionSpec as P

MESH = pl.DeviceIdType.MESH
F32 = jnp.float32
BF16 = jnp.bfloat16
WIDE = 24
LANES = 128


def iota(shape, dim):
    return lax.broadcasted_iota(jnp.int32, shape, dim)


def kernel(
    n, cap, tokens, chunk, chunks, quarter,
    grad_ref, routes_ref, gate_ref, hidden_ref, weight_ref,
    own_ref, other_ref, hg_ref, prob_ref,
    tok, meta, onehot_t0, onehot_t1, onehot, send0, recv0, send, recv,
    wbuf, hid_all, hid_part, hid_rows, hid_t, q,
    dg_own, dg_send, hg_own, hg_send, part_out, part_in, back_out, back_in,
    load_sem, tok_ssem, tok_rsem, meta_ssem, meta_rsem, hid_ssem, hid_rsem,
    w_ssem, w_rsem, row_ssem, row_rsem, dg_ssem, dg_rsem, out_sem,
    hg_ssem, hg_rsem, part_ssem, part_rsem, back_ssem, back_rsem,
):
    d, e = lax.axis_index("dp"), lax.axis_index("expert")
    zl, i = e // n, e % n
    across = (1 - zl) * n + i
    da = 3 - d
    hq = d % 2
    db = d + 1 - 2 * hq
    hh = d // 2
    half = 2 * quarter
    span = 2 * WIDE
    rows = n * span
    slots = 2 * n * cap
    mine = pl.multiple_of(i * span, span)

    def remote(src, dst, ssem, rsem, device):
        return pltpu.make_async_remote_copy(
            src_ref=src, dst_ref=dst, send_sem=ssem, recv_sem=rsem,
            device_id=device, device_id_type=MESH,
        )

    def columns(k):
        return pl.ds(k * chunk, chunk)

    own_block = pl.multiple_of(zl * tokens, tokens)
    own_rows = pl.multiple_of(hq * quarter, quarter)
    tok_loads = [
        pltpu.make_async_copy(
            grad_ref.at[:, columns(k)], tok.at[k, pl.ds(own_block, tokens)], load_sem.at[k]
        )
        for k in range(chunks)
    ]
    w_loads = [
        pltpu.make_async_copy(
            weight_ref.at[:, columns(k)], wbuf.at[k, pl.ds(own_rows, quarter)], load_sem.at[chunks + k]
        )
        for k in range(chunks)
    ]
    hid_load = pltpu.make_async_copy(hidden_ref, hid_all, load_sem.at[2 * chunks])
    for load in tok_loads + [hid_load] + w_loads:
        load.start()

    barrier = pltpu.get_barrier_semaphore()

    def greet(j, carry):
        pl.semaphore_signal(
            barrier, inc=1, device_id=(d, (e + j) % (2 * n)), device_id_type=MESH
        )
        return carry

    lax.fori_loop(1, 2 * n, greet, 0)
    for device in ((da, e), (da, across), (db, e)):
        pl.semaphore_signal(barrier, inc=1, device_id=device, device_id_type=MESH)
    pl.semaphore_wait(barrier, 2 * n + 2)

    def token_copies(k):
        here = tok.at[k, pl.ds(own_block, tokens)]
        there = tok.at[k, pl.ds(pl.multiple_of((2 + zl) * tokens, tokens), tokens)]
        return [
            remote(here, here, tok_ssem.at[k, 0], tok_rsem.at[k, 0], (d, across)),
            remote(here, there, tok_ssem.at[k, 1], tok_rsem.at[k, 1], (da, e)),
            remote(here, there, tok_ssem.at[k, 2], tok_rsem.at[k, 2], (da, across)),
        ]

    def send_tokens(k):
        tok_loads[k].wait()
        for copy in token_copies(k):
            copy.start()

    send_tokens(0)

    experts = routes_ref[...]
    lane = iota((tokens, LANES), 1)
    name0, name1 = experts[:, 0:1], experts[:, 1:2]
    member0 = (lane == name0).astype(F32)
    member1 = (lane == name1).astype(F32)
    before = (iota((tokens, tokens), 1) < iota((tokens, tokens), 0)).astype(F32).astype(BF16)
    earlier = jnp.dot(before, (member0 + member1).astype(BF16), preferred_element_type=F32)
    slot0 = jnp.sum(earlier * member0, axis=1, keepdims=True)
    slot1 = jnp.sum(earlier * member1, axis=1, keepdims=True)
    gates = gate_ref[...].astype(F32)
    place0 = name0.astype(F32) * span + slot0
    place1 = name1.astype(F32) * span + slot1
    info = jnp.where(lane == 0, place0, 0.0)
    info = jnp.where(lane == 1, place1, info)
    info = jnp.where(lane == 2, gates[:, 0:1], info)
    info = jnp.where(lane == 3, gates[:, 1:2], info)
    meta[pl.ds(own_block, tokens), :] = info
    meta_here = meta.at[pl.ds(own_block, tokens)]
    meta_there = meta.at[pl.ds(pl.multiple_of((2 + zl) * tokens, tokens), tokens)]
    meta_copies = [
        remote(meta_here, meta_here, meta_ssem.at[0], meta_rsem.at[0], (d, across)),
        remote(meta_here, meta_there, meta_ssem.at[1], meta_rsem.at[1], (da, e)),
        remote(meta_here, meta_there, meta_ssem.at[2], meta_rsem.at[2], (da, across)),
    ]
    for copy in meta_copies:
        copy.start()
    send_tokens(1)

    hid_load.wait()
    hid_copy = remote(
        hid_all.at[:, pl.ds(pl.multiple_of((1 - hh) * half, half), half)],
        hid_part, hid_ssem, hid_rsem, (da, e),
    )
    hid_copy.start()
    for k in range(2, min(4, chunks)):
        send_tokens(k)

    for copy in meta_copies:
        copy.wait_recv()
    row_lane = iota((tokens, rows), 1).astype(F32)
    plane = (zl * rows).astype(F32)
    for block in range(4):
        part = pl.ds(block * tokens, tokens)
        offset = float((block // 2) * WIDE + (block % 2) * cap)
        seen = meta[part, :]
        onehot_t0[part, :] = (row_lane == seen[:, 0:1] - plane + offset).astype(F32).astype(BF16)
        onehot_t1[part, :] = (row_lane == seen[:, 1:2] - plane + offset).astype(F32).astype(BF16)

    tile = min(LANES, rows)

    def flip(t, carry):
        part = pl.ds(pl.multiple_of(t * tile, tile), tile)
        first = onehot_t0[:, part].T
        second = onehot_t1[:, part].T
        onehot[part, :] = first + second
        gate0 = jnp.broadcast_to(meta[:, 2:3], (4 * tokens, LANES)).astype(BF16)
        gate1 = jnp.broadcast_to(meta[:, 3:4], (4 * tokens, LANES)).astype(BF16)
        gate = jnp.dot(first, gate0, preferred_element_type=F32)
        gate = gate + jnp.dot(second, gate1, preferred_element_type=F32)
        send0[part, pl.ds(chunk, LANES)] = gate.astype(BF16)
        return carry

    lax.fori_loop(0, rows // tile, flip, 0)

    def buffers(k):
        return (send0, recv0) if k == 0 else (send.at[k - 1], recv.at[k - 1])

    pack = min(8, n)

    def gather(k):
        for copy in token_copies(k):
            copy.wait_recv()
        out, into = buffers(k)

        def step(s, carry):
            group = (i // pack + s) % (n // pack)
            part = pl.ds(pl.multiple_of(group * (pack * span), pack * span), pack * span)
            out[part, pl.ds(0, chunk)] = jnp.dot(
                onehot[part, :], tok[k], preferred_element_type=F32
            ).astype(BF16)

            def issue(j, inner):
                to = group * pack + (i + j) % pack

                @pl.when(to != i)
                def _():
                    remote(
                        out.at[pl.ds(pl.multiple_of(to * span, span), span)],
                        into.at[pl.ds(mine, span)],
                        row_ssem.at[k], row_rsem.at[k], (d, zl * n + to),
                    ).start()

                return inner

            return lax.fori_loop(0, pack, issue, carry)

        lax.fori_loop(0, n // pack, step, 0)
        into[pl.ds(mine, span), :] = out[pl.ds(mine, span), :]

    def row_wait(k):
        out, into = buffers(k)
        many = pl.ds(0, (n - 1) * span)
        return remote(out.at[many], into.at[many], row_ssem.at[k], row_rsem.at[k], (db, e))

    w_copies = [
        remote(
            wbuf.at[k, pl.ds(own_rows, quarter)], wbuf.at[k, pl.ds(own_rows, quarter)],
            w_ssem.at[k], w_rsem.at[k], (db, e),
        )
        for k in range(chunks)
    ]
    dg_copies = [
        remote(dg_send.at[k], other_ref.at[:, columns(k)], dg_ssem.at[k], dg_rsem.at[k], (db, e))
        for k in range(chunks)
    ]
    own_copies = [
        pltpu.make_async_copy(dg_own.at[k], own_ref.at[:, columns(k)], out_sem.at[k])
        for k in range(chunks)
    ]

    def order_hidden():
        hid_copy.wait_recv()
        at = iota((n * WIDE, slots), 1)
        source = at % (2 * n)
        target = (source % n) * WIDE + (source // n) * cap + at // (2 * n)
        order = (iota((n * WIDE, slots), 0) == target).astype(F32).astype(BF16)
        near = hid_all[:, pl.ds(pl.multiple_of(hh * half, half), half)]
        near = jnp.dot(order, near, preferred_element_type=F32).reshape(n, 1, WIDE, half)
        far = jnp.dot(order, hid_part[...], preferred_element_type=F32).reshape(n, 1, WIDE, half)
        both = jnp.concatenate([near, far], axis=1).reshape(rows, half)
        hid_rows[...] = both.astype(BF16)

    def weigh_hidden():
        def turn(t, carry):
            part = pl.ds(pl.multiple_of(t * tile, tile), tile)
            gate = recv0[part, pl.ds(chunk, LANES)].astype(F32)[:, 0:1]
            hid_t[:, part] = (hid_rows[part, :].astype(F32) * gate).astype(BF16).T
            return carry

        lax.fori_loop(0, rows // tile, turn, 0)

    def down(k):
        row_wait(k).wait_recv()
        if k == 0:
            weigh_hidden()
        into = buffers(k)[1]
        got = into[:, pl.ds(0, chunk)]
        theirs = pl.ds(pl.multiple_of((1 - hq) * quarter, quarter), quarter)
        dg_send[k] = jnp.dot(hid_t[theirs, :], got, preferred_element_type=F32).astype(BF16)
        dg_copies[k].start()
        dg_own[k] = jnp.dot(hid_t[pl.ds(own_rows, quarter), :], got, preferred_element_type=F32)
        own_copies[k].start()

    strip = rows // 6

    def project(k):
        w_copies[k].wait_recv()
        into = buffers(k)[1]

        def step(t, carry):
            part = pl.ds(pl.multiple_of(t * strip, strip), strip)
            more = lax.dot_general(
                into[part, pl.ds(0, chunk)], wbuf[k], (((1,), (1,)), ((), ())),
                preferred_element_type=F32,
            )
            q[part, :] = more if k == 0 else q[part, :] + more
            return carry

        lax.fori_loop(0, 6, step, 0)

    lag = min(3, chunks - 1)
    for k in range(chunks):
        gather(k)
        if k + 4 < chunks:
            send_tokens(k + 4)
        w_loads[k].wait()
        w_copies[k].start()
        if k == 0:
            order_hidden()
        if k >= 1:
            down(k - 1)
        if k >= 1 + lag:
            project(k - 1 - lag)
    down(chunks - 1)
    for k in range(chunks - 1 - lag, chunks):
        project(k)

    gate = recv0[:, pl.ds(chunk, LANES)].astype(F32)[:, 0:1]
    product = q[...]
    scaled = (product * gate).reshape(n, 2, WIDE, half)
    source = iota((slots, n * WIDE), 0)
    target = (source % n) * WIDE + (source % (2 * n)) // n * cap + source // (2 * n)
    order = (iota((slots, n * WIDE), 1) == target).astype(F32).astype(BF16)
    far = scaled[:, 1].reshape(n * WIDE, half).astype(BF16)
    hg_send[...] = jnp.dot(order, far, preferred_element_type=F32).astype(BF16)
    hg_columns = pl.ds(pl.multiple_of(hh * half, half), half)
    hg_copy = remote(hg_send, hg_ref.at[:, hg_columns], hg_ssem, hg_rsem, (da, e))
    hg_copy.start()
    sums = jnp.sum(hid_rows[...].astype(F32) * product, axis=1, keepdims=True)
    spread = jnp.where(
        iota((rows, LANES), 1) == iota((rows, LANES), 0) % WIDE, sums, 0.0
    ).reshape(n, 2, WIDE, LANES)
    spread = jnp.sum(spread, axis=2)
    part_out[...] = spread[:, 1]
    part_copy = remote(part_out, part_in, part_ssem, part_rsem, (da, e))
    part_copy.start()
    near = scaled[:, 0].reshape(n * WIDE, half).astype(BF16)
    hg_own[...] = jnp.dot(order, near, preferred_element_type=F32).astype(BF16)
    hg_store = pltpu.make_async_copy(hg_own, hg_ref.at[:, hg_columns], out_sem.at[chunks])
    hg_store.start()
    part_copy.wait_recv()
    total = spread[:, 0] + part_in[...]
    back_out[...] = jnp.broadcast_to(total[:, None, :], (n, 8, LANES))

    def give(j, carry):
        to = (e + j) % (2 * n)
        remote(
            back_out.at[to % n], back_in.at[e], back_ssem, back_rsem, (d, to)
        ).start()
        return carry

    lax.fori_loop(1, 2 * n, give, 0)
    back_in[e] = back_out[i]
    many = pl.ds(0, 2 * n - 1)
    remote(back_in.at[many], back_in.at[many], back_ssem, back_rsem, (db, e)).wait()
    table = back_in[...][:, 0, :]
    for k, (member, slot) in enumerate(((member0, slot0), (member1, slot1))):
        found = jnp.dot(
            member[:, : 2 * n], table, preferred_element_type=F32, precision=lax.Precision.HIGHEST
        )
        at = slot + (zl * cap).astype(F32)
        value = jnp.sum(jnp.where(lane.astype(F32) == at, found, 0.0), axis=1, keepdims=True)
        prob_ref[:, k : k + 1] = value

    for k in range(chunks):
        for copy in token_copies(k):
            copy.wait_send()
        w_copies[k].wait_send()
        row_wait(k).wait_send()
        dg_copies[k].wait()
        own_copies[k].wait()
    for copy in meta_copies:
        copy.wait_send()
    hid_copy.wait_send()
    part_copy.wait_send()
    hg_copy.wait()
    hg_store.wait()


def per_device(grad_out, routes, route_weight, hidden_saved, down_weight):
    tokens, width = grad_out.shape
    n = lax.axis_size("expert") // 2
    cap, hidden_width = hidden_saved.shape[3], hidden_saved.shape[4]
    quarter = down_weight.shape[1]
    half = 2 * quarter
    chunks = 7
    chunk = width // chunks
    rows = n * 2 * WIDE
    slots = 2 * n * cap
    hidden = hidden_saved.reshape(2 * n, cap, hidden_width).transpose(1, 0, 2)
    vmem = pl.BlockSpec(memory_space=pltpu.VMEM)
    anywhere = pl.BlockSpec(memory_space=pl.ANY)
    sem = pltpu.SemaphoreType.DMA
    flops = 2 * rows * width * (4 * tokens + half + half)
    own, other, hidden_grad, prob_grad = pl.pallas_call(
        functools.partial(kernel, n, cap, tokens, chunk, chunks, quarter),
        out_shape=(
            jax.ShapeDtypeStruct((quarter, width), F32),
            jax.ShapeDtypeStruct((quarter, width), BF16),
            jax.ShapeDtypeStruct((slots, hidden_width), BF16),
            jax.ShapeDtypeStruct((tokens, 2), F32),
        ),
        in_specs=[anywhere, vmem, vmem, anywhere, anywhere],
        out_specs=(anywhere, anywhere, anywhere, vmem),
        scratch_shapes=[
            pltpu.VMEM((chunks, 4 * tokens, chunk), BF16),
            pltpu.VMEM((4 * tokens, LANES), F32),
            pltpu.VMEM((4 * tokens, rows), BF16),
            pltpu.VMEM((4 * tokens, rows), BF16),
            pltpu.VMEM((rows, 4 * tokens), BF16),
            pltpu.VMEM((rows, chunk + LANES), BF16),
            pltpu.VMEM((rows, chunk + LANES), BF16),
            pltpu.VMEM((chunks - 1, rows, chunk), BF16),
            pltpu.VMEM((chunks - 1, rows, chunk), BF16),
            pltpu.VMEM((chunks, half, chunk), BF16),
            pltpu.VMEM((slots, hidden_width), BF16),
            pltpu.VMEM((slots, half), BF16),
            pltpu.VMEM((rows, half), BF16),
            pltpu.VMEM((half, rows), BF16),
            pltpu.VMEM((rows, half), F32),
            pltpu.VMEM((chunks, quarter, chunk), F32),
            pltpu.VMEM((chunks, quarter, chunk), BF16),
            pltpu.VMEM((slots, half), BF16),
            pltpu.VMEM((slots, half), BF16),
            pltpu.VMEM((n, LANES), F32),
            pltpu.VMEM((n, LANES), F32),
            pltpu.VMEM((n, 8, LANES), F32),
            pltpu.VMEM((2 * n, 8, LANES), F32),
            sem((2 * chunks + 1,)),
            sem((chunks, 3)),
            sem((chunks, 3)),
            sem((3,)),
            sem((3,)),
            sem,
            sem,
            sem((chunks,)),
            sem((chunks,)),
            sem((chunks,)),
            sem((chunks,)),
            sem((chunks,)),
            sem((chunks,)),
            sem((chunks + 1,)),
            sem,
            sem,
            sem,
            sem,
            sem,
            sem,
        ],
        compiler_params=pltpu.CompilerParams(
            collective_id=0, has_side_effects=True, vmem_limit_bytes=62 * 1024 * 1024
        ),
        cost_estimate=pl.CostEstimate(flops=flops, bytes_accessed=1 << 24, transcendentals=0),
    )(
        grad_out,
        routes,
        route_weight,
        hidden.reshape(slots, hidden_width),
        down_weight.reshape(quarter, width),
    )
    down_grad = own + other.astype(F32)
    hidden_grad = hidden_grad.reshape(cap, 2 * n, hidden_width).transpose(1, 0, 2)
    return (
        down_grad.reshape(1, quarter, width),
        hidden_grad.reshape(hidden_saved.shape),
        prob_grad,
    )


def solution(mesh):
    placed = (
        P(("dp", "expert"), None),
        P(("dp", "expert"), None),
        P(("dp", "expert"), None),
        P("expert", "dp", None, None, None),
        P("expert", "dp", None),
    )
    return jax.shard_map(
        per_device,
        mesh=mesh,
        in_specs=placed,
        out_specs=(
            P("expert", "dp", None),
            P("expert", "dp", None, None, None),
            P(("dp", "expert"), None),
        ),
        check_vma=False,
    )
```

time: 437 us -> 285 us (0.65)
  waiting for transfers between devices: 284 us -> 0 us
  Pallas kernels: 0 us -> 274 us
  local copies, waits for them, and re-layouts: 60.5 us -> 4.57 us
  matrix products: 34 us -> 0 us
  starting transfers between devices: 28 us -> 0 us
  between operations: 14.2 us -> 0.66 us
  other arithmetic: 14.9 us -> 4.98 us
    pallas_call x0 -> x1, Pallas kernels: none -> 274 us  [per_device(): pl.pallas_call(functools.partial(kernel, n, cap, tokens, chunk, chunks, q...]
    all_to_all x3 -> x0, waiting for transfers between devices: 197 us -> none  [the longest x1 197 us: per_device(): lax.all_to_all(send_rows.reshape(expert_count, capacity, model_width), 'e...]
    reduce_scatter x1 -> x0, waiting for transfers between devices: 85.5 us -> none  [per_device(): lax.psum_scatter(lax.dot_general(columns, scaled, contract_first, preferr...]
    dot_general x3 -> x0, matrix products: 34 us -> none  [the longest x1 12 us: per_device(): output_sum = jnp.dot(columns, piece, preferred_element_type=jnp.float32)]
    all_to_all x3 -> x0, starting transfers between devices: 27.9 us -> none  [the longest x1 10.4 us: per_device(): lax.all_to_all(send_weights.reshape(expert_count, capacity), 'expert', sp...]
    convert_element_type x3 -> x0, local copies, waits for them, and re-layouts: 17.2 us -> none  [the longest x2 17.1 us: per_device(): scaled = (slot_weights * sent_rows.astype(jnp.float32)).astype(jnp.bfloat16)]
    scatter x2 -> x0, local copies, waits for them, and re-layouts: 15.8 us -> none  [the longest x1 13.2 us: per_device(): send_rows = jnp.zeros((slot_total, model_width), jnp.bfloat16).at[destina...]
    reshape x6 -> x0, local copies, waits for them, and re-layouts: 11.8 us -> none  [the longest x1 7.67 us: per_device(): send_rows.reshape(expert_count, capacity, model_width)]
  transfers between devices with their start and end apart: 5 -> 0, of which waited for: 2 -> 0; matrix products, arithmetic and copies ran while one was open for 21% -> 0% of each run, Pallas kernels for 0% -> 0%
where the time goes in v1:
time: 285 us
  Pallas kernels  274 us (96%)
  other arithmetic  4.98 us (2%)
  local copies, waits for them, and re-layouts  4.57 us (2%)
    pallas_call x1, Pallas kernels, per_device(): pl.pallas_call(functools.partial(kernel, n, cap, tokens, chunk, chunks, q...  274 us

profile of v1, /device:TPU:1, one launch (start us, length us, event | category | flops | bytes accessed | tf_op | source)
XLA Modules:
  0.0 284.7 jit_solution(4940096827652895462)
XLA Ops:
  0.6 1.4 copy.9.gate_ref
  2.0 1.4 copy.8.routes_ref
  3.5 274.5 %shard_map.76 = (f32[256,3584]{1,0:T(8,128)}, bf16[256,3584]{1,0:T(8,128)(2,1)}, bf16[640,1024]{1,0:T(8,128)(2,1)}, f32[160,2]{1,0:T(8,128)}) custom-call(bf16[160,3584]{1,0:T(8,128)(2,1)} %grad_ref.1, s32[160,2]{1,0:T(8,128)} %copy.8.routes_ref, bf16[160,2]{1,0:T(8,128)(2,1)} %copy.9.gate_ref, bf16[640,1024]{1,0:T(8,128)(2,1)} %bitcast.15, ...), custom_call_target="tpu_custom_call" | custom-call | flops 18320719872 | bytes 16777216 | tf_op jit(solution)/shard_map/pallas_call | solution.py:365
  277.9 0.0 copy-start.1
  278.0 0.0 copy-start
  278.0 5.0 %add_bitcast_fusion = f32[1,256,3584]{2,1,0:T(8,128)} fusion(f32[256,3584]{1,0:T(8,128)} %get-tuple-element.7, bf16[256,3584]{1,0:T(8,128)(2,1)} %get-tuple-element.8), kind=kLoop, calls=%fused_computation | loop fusion | flops 1835008 | bytes 9175040 | tf_op jit(solution)/shard_map/reshape | solution.py:434
  282.9 0.0 copy-done.1
  283.0 0.7 copy.10
  283.6 0.0 copy-done
  283.6 1.1 copy.12
Async XLA Ops:
  277.9 5.0 %copy-start.1 = (f32[160,2]{1,0:T(8,128)S(1)}, f32[160,2]{1,0:T(8,128)}, u32[]{:S(2)}) copy-start(f32[160,2]{1,0:T(8,128)} %get-tuple-element.13) | copy-start | bytes 3844
  278.0 5.7 %copy-start = (bf16[640,1024]{1,0:T(8,128)(2,1)S(1)}, bf16[640,1024]{1,0:T(8,128)(2,1)}, u32[]{:S(2)}) copy-start(bf16[640,1024]{1,0:T(8,128)(2,1)} %get-tuple-element.9) | copy-start | bytes 3932164

commit v2 on v1

--- a/solution.py
+++ b/solution.py
@@ -22,7 +22,7 @@
     n, cap, tokens, chunk, chunks, quarter,
     grad_ref, routes_ref, gate_ref, hidden_ref, weight_ref,
     own_ref, other_ref, hg_ref, prob_ref,
-    tok, meta, onehot_t0, onehot_t1, onehot, send0, recv0, send, recv,
+    tok, meta, place0, place1, onehot, order_back, send0, recv0, send, recv,
     wbuf, hid_all, hid_part, hid_rows, hid_t, q,
     dg_own, dg_send, hg_own, hg_send, part_out, part_in, back_out, back_in,
     load_sem, tok_ssem, tok_rsem, meta_ssem, meta_rsem, hid_ssem, hid_rsem,
@@ -82,39 +82,74 @@
         pl.semaphore_signal(barrier, inc=1, device_id=device, device_id_type=MESH)
     pl.semaphore_wait(barrier, 2 * n + 2)
 
+    inner = zl == hq
+    far_blocks = pl.ds(2 * tokens, 2 * tokens)
+
     def token_copies(k):
         here = tok.at[k, pl.ds(own_block, tokens)]
         there = tok.at[k, pl.ds(pl.multiple_of((2 + zl) * tokens, tokens), tokens)]
-        return [
+        both = tok.at[k, far_blocks]
+        return (
             remote(here, here, tok_ssem.at[k, 0], tok_rsem.at[k, 0], (d, across)),
-            remote(here, there, tok_ssem.at[k, 1], tok_rsem.at[k, 1], (da, e)),
-            remote(here, there, tok_ssem.at[k, 2], tok_rsem.at[k, 2], (da, across)),
-        ]
+            remote(here, there, tok_ssem.at[k, 1], tok_rsem.at[k, 1], (da, across)),
+            remote(here, there, tok_ssem.at[k, 1], tok_rsem.at[k, 2], (da, e)),
+            remote(both, both, tok_ssem.at[k, 2], tok_rsem.at[k, 3], (d, across)),
+        )
 
     def send_tokens(k):
         tok_loads[k].wait()
-        for copy in token_copies(k):
-            copy.start()
+        beside, near, far, _ = token_copies(k)
+        beside.start()
+        pl.when(inner)(near.start)
+        pl.when(jnp.logical_not(inner))(far.start)
+
+    def hand_on(k):
+        _, near, far, both = token_copies(k)
+
+        @pl.when(inner)
+        def _():
+            near.wait_recv()
+            far.wait_recv()
+            both.start()
+
+    def await_tokens(k):
+        beside, _, _, both = token_copies(k)
+        beside.wait_recv()
+        pl.when(jnp.logical_not(inner))(both.wait_recv)
+
+    def end_tokens(k):
+        beside, near, _, both = token_copies(k)
+        beside.wait_send()
+        near.wait_send()
+        pl.when(inner)(both.wait_send)
 
     send_tokens(0)
 
-    experts = routes_ref[...]
     lane = iota((tokens, LANES), 1)
-    name0, name1 = experts[:, 0:1], experts[:, 1:2]
-    member0 = (lane == name0).astype(F32)
-    member1 = (lane == name1).astype(F32)
+    lane_f = lane.astype(F32)
+
+    def column(array, k):
+        pick = (iota((2, LANES), 0) == k).astype(F32).astype(BF16)
+        return lax.dot_general(
+            array, pick, (((0,), (0,)), ((), ())), preferred_element_type=F32
+        )
+
+    experts = routes_ref[...].astype(F32).astype(BF16)
+    name0, name1 = column(experts, 0), column(experts, 1)
+    member0 = (lane_f == name0).astype(F32)
+    member1 = (lane_f == name1).astype(F32)
     before = (iota((tokens, tokens), 1) < iota((tokens, tokens), 0)).astype(F32).astype(BF16)
     earlier = jnp.dot(before, (member0 + member1).astype(BF16), preferred_element_type=F32)
     slot0 = jnp.sum(earlier * member0, axis=1, keepdims=True)
     slot1 = jnp.sum(earlier * member1, axis=1, keepdims=True)
-    gates = gate_ref[...].astype(F32)
-    place0 = name0.astype(F32) * span + slot0
-    place1 = name1.astype(F32) * span + slot1
-    info = jnp.where(lane == 0, place0, 0.0)
-    info = jnp.where(lane == 1, place1, info)
-    info = jnp.where(lane == 2, gates[:, 0:1], info)
-    info = jnp.where(lane == 3, gates[:, 1:2], info)
-    meta[pl.ds(own_block, tokens), :] = info
+    gates = gate_ref[...]
+    info = jnp.where(lane == 0, name0, 0.0)
+    info = jnp.where(lane == 1, name1, info)
+    info = jnp.where(lane == 2, column(gates, 0), info)
+    info = jnp.where(lane == 3, column(gates, 1), info)
+    info = jnp.where(lane == 4, slot0, info)
+    info = jnp.where(lane == 5, slot1, info)
+    meta[pl.ds(own_block, tokens), :] = info.astype(BF16)
     meta_here = meta.at[pl.ds(own_block, tokens)]
     meta_there = meta.at[pl.ds(pl.multiple_of((2 + zl) * tokens, tokens), tokens)]
     meta_copies = [
@@ -132,69 +167,86 @@
         hid_part, hid_ssem, hid_rsem, (da, e),
     )
     hid_copy.start()
-    for k in range(2, min(4, chunks)):
-        send_tokens(k)
+    send_tokens(2)
+
+    to = iota((slots, n * WIDE), 0)
+    to = (to % n) * WIDE + (to % (2 * n)) // n * cap + to // (2 * n)
+    order_back[...] = (iota((slots, n * WIDE), 1) == to).astype(F32).astype(BF16)
+    hand_on(0)
 
     for copy in meta_copies:
         copy.wait_recv()
-    row_lane = iota((tokens, rows), 1).astype(F32)
     plane = (zl * rows).astype(F32)
     for block in range(4):
         part = pl.ds(block * tokens, tokens)
         offset = float((block // 2) * WIDE + (block % 2) * cap)
-        seen = meta[part, :]
-        onehot_t0[part, :] = (row_lane == seen[:, 0:1] - plane + offset).astype(F32).astype(BF16)
-        onehot_t1[part, :] = (row_lane == seen[:, 1:2] - plane + offset).astype(F32).astype(BF16)
+        seen = meta[part, :].astype(F32)
+        at = seen[:, 0:1] * span + seen[:, 4:5] - plane + offset
+        place0[part, :] = jnp.broadcast_to(at, (tokens, LANES))
+        at = seen[:, 1:2] * span + seen[:, 5:6] - plane + offset
+        place1[part, :] = jnp.broadcast_to(at, (tokens, LANES))
 
     tile = min(LANES, rows)
 
-    def flip(t, carry):
+    def build(t, carry):
         part = pl.ds(pl.multiple_of(t * tile, tile), tile)
-        first = onehot_t0[:, part].T
-        second = onehot_t1[:, part].T
-        onehot[part, :] = first + second
-        gate0 = jnp.broadcast_to(meta[:, 2:3], (4 * tokens, LANES)).astype(BF16)
-        gate1 = jnp.broadcast_to(meta[:, 3:4], (4 * tokens, LANES)).astype(BF16)
+        row = (iota((4 * tokens, LANES), 1) + t * tile).astype(F32)
+        first = (place0[...] == row).astype(F32).astype(BF16).T
+        second = (place1[...] == row).astype(F32).astype(BF16).T
+        onehot[part, :] = (first + second)[:tile]
+        gate0 = jnp.broadcast_to(meta[:, 2:3], (4 * tokens, LANES))
+        gate1 = jnp.broadcast_to(meta[:, 3:4], (4 * tokens, LANES))
         gate = jnp.dot(first, gate0, preferred_element_type=F32)
         gate = gate + jnp.dot(second, gate1, preferred_element_type=F32)
-        send0[part, pl.ds(chunk, LANES)] = gate.astype(BF16)
+        send0[part, pl.ds(chunk, LANES)] = gate[:tile].astype(BF16)
         return carry
-
-    lax.fori_loop(0, rows // tile, flip, 0)
 
     def buffers(k):
         return (send0, recv0) if k == 0 else (send.at[k - 1], recv.at[k - 1])
 
     pack = min(8, n)
 
+    group_rows = pack * span
+    tiles = max(1, group_rows // tile)
+
+    def message(k, to):
+        out, into = buffers(k)
+
+        @pl.when(to != i)
+        def _():
+            remote(
+                out.at[pl.ds(pl.multiple_of(to * span, span), span)],
+                into.at[pl.ds(mine, span)],
+                row_ssem.at[k], row_rsem.at[k], (d, zl * n + to),
+            ).start()
+
     def gather(k):
-        for copy in token_copies(k):
-            copy.wait_recv()
+        await_tokens(k)
         out, into = buffers(k)
 
         def step(s, carry):
             group = (i // pack + s) % (n // pack)
-            part = pl.ds(pl.multiple_of(group * (pack * span), pack * span), pack * span)
+            if k == 0:
+                lax.fori_loop(group * tiles, group * tiles + tiles, build, 0)
+            part = pl.ds(pl.multiple_of(group * group_rows, group_rows), group_rows)
             out[part, pl.ds(0, chunk)] = jnp.dot(
                 onehot[part, :], tok[k], preferred_element_type=F32
             ).astype(BF16)
 
-            def issue(j, inner):
-                to = group * pack + (i + j) % pack
-
-                @pl.when(to != i)
-                def _():
-                    remote(
-                        out.at[pl.ds(pl.multiple_of(to * span, span), span)],
-                        into.at[pl.ds(mine, span)],
-                        row_ssem.at[k], row_rsem.at[k], (d, zl * n + to),
-                    ).start()
-
-                return inner
-
-            return lax.fori_loop(0, pack, issue, carry)
+            def issue(j, inner_carry):
+                message(k, group * pack + (i + j) % pack)
+                return inner_carry
+
+            return lax.fori_loop(0, pack, issue, carry) if k == 0 else carry
 
         lax.fori_loop(0, n // pack, step, 0)
+
+        def issue(j, carry):
+            message(k, (i + 5 * j) % n)
+            return carry
+
+        if k > 0:
+            lax.fori_loop(1, n, issue, 0)
         into[pl.ds(mine, span), :] = out[pl.ds(mine, span), :]
 
     def row_wait(k):
@@ -240,7 +292,8 @@
         lax.fori_loop(0, rows // tile, turn, 0)
 
     def down(k):
-        row_wait(k).wait_recv()
+        if k < chunks - 1:
+            row_wait(k).wait_recv()
         if k == 0:
             weigh_hidden()
         into = buffers(k)[1]
@@ -268,35 +321,35 @@
 
         lax.fori_loop(0, 6, step, 0)
 
-    lag = min(3, chunks - 1)
     for k in range(chunks):
+        if k + 1 < chunks:
+            hand_on(k + 1)
         gather(k)
-        if k + 4 < chunks:
-            send_tokens(k + 4)
+        if k + 3 < chunks:
+            send_tokens(k + 3)
         w_loads[k].wait()
         w_copies[k].start()
         if k == 0:
             order_hidden()
         if k >= 1:
             down(k - 1)
-        if k >= 1 + lag:
-            project(k - 1 - lag)
-    down(chunks - 1)
-    for k in range(chunks - 1 - lag, chunks):
-        project(k)
-
-    gate = recv0[:, pl.ds(chunk, LANES)].astype(F32)[:, 0:1]
-    product = q[...]
-    scaled = (product * gate).reshape(n, 2, WIDE, half)
-    source = iota((slots, n * WIDE), 0)
-    target = (source % n) * WIDE + (source % (2 * n)) // n * cap + source // (2 * n)
-    order = (iota((slots, n * WIDE), 1) == target).astype(F32).astype(BF16)
-    far = scaled[:, 1].reshape(n * WIDE, half).astype(BF16)
-    hg_send[...] = jnp.dot(order, far, preferred_element_type=F32).astype(BF16)
+            project(k - 1)
+
+    row_wait(chunks - 1).wait_recv()
+    project(chunks - 1)
     hg_columns = pl.ds(pl.multiple_of(hh * half, half), half)
     hg_copy = remote(hg_send, hg_ref.at[:, hg_columns], hg_ssem, hg_rsem, (da, e))
+    hg_store = pltpu.make_async_copy(hg_own, hg_ref.at[:, hg_columns], out_sem.at[chunks])
+
+    def weigh(g):
+        gate = recv0[:, pl.ds(chunk, LANES)].astype(F32)[:, 0:1].reshape(n, 2, WIDE, 1)[:, g]
+        got = q[...].reshape(n, 2, WIDE, half)[:, g]
+        got = (got * gate).reshape(n * WIDE, half).astype(BF16)
+        return jnp.dot(order_back[...], got, preferred_element_type=F32).astype(BF16)
+
+    hg_send[...] = weigh(1)
     hg_copy.start()
-    sums = jnp.sum(hid_rows[...].astype(F32) * product, axis=1, keepdims=True)
+    sums = jnp.sum(hid_rows[...].astype(F32) * q[...], axis=1, keepdims=True)
     spread = jnp.where(
         iota((rows, LANES), 1) == iota((rows, LANES), 0) % WIDE, sums, 0.0
     ).reshape(n, 2, WIDE, LANES)
@@ -304,9 +357,8 @@
     part_out[...] = spread[:, 1]
     part_copy = remote(part_out, part_in, part_ssem, part_rsem, (da, e))
     part_copy.start()
-    near = scaled[:, 0].reshape(n * WIDE, half).astype(BF16)
-    hg_own[...] = jnp.dot(order, near, preferred_element_type=F32).astype(BF16)
-    hg_store = pltpu.make_async_copy(hg_own, hg_ref.at[:, hg_columns], out_sem.at[chunks])
+    down(chunks - 1)
+    hg_own[...] = weigh(0)
     hg_store.start()
     part_copy.wait_recv()
     total = spread[:, 0] + part_in[...]
@@ -329,12 +381,11 @@
             member[:, : 2 * n], table, preferred_element_type=F32, precision=lax.Precision.HIGHEST
         )
         at = slot + (zl * cap).astype(F32)
-        value = jnp.sum(jnp.where(lane.astype(F32) == at, found, 0.0), axis=1, keepdims=True)
+        value = jnp.sum(jnp.where(lane_f == at, found, 0.0), axis=1, keepdims=True)
         prob_ref[:, k : k + 1] = value
 
     for k in range(chunks):
-        for copy in token_copies(k):
-            copy.wait_send()
+        end_tokens(k)
         w_copies[k].wait_send()
         row_wait(k).wait_send()
         dg_copies[k].wait()
@@ -374,10 +425,11 @@
         out_specs=(anywhere, anywhere, anywhere, vmem),
         scratch_shapes=[
             pltpu.VMEM((chunks, 4 * tokens, chunk), BF16),
+            pltpu.VMEM((4 * tokens, LANES), BF16),
             pltpu.VMEM((4 * tokens, LANES), F32),
-            pltpu.VMEM((4 * tokens, rows), BF16),
-            pltpu.VMEM((4 * tokens, rows), BF16),
+            pltpu.VMEM((4 * tokens, LANES), F32),
             pltpu.VMEM((rows, 4 * tokens), BF16),
+            pltpu.VMEM((slots, n * WIDE), BF16),
             pltpu.VMEM((rows, chunk + LANES), BF16),
             pltpu.VMEM((rows, chunk + LANES), BF16),
             pltpu.VMEM((chunks - 1, rows, chunk), BF16),
@@ -398,7 +450,7 @@
             pltpu.VMEM((2 * n, 8, LANES), F32),
             sem((2 * chunks + 1,)),
             sem((chunks, 3)),
-            sem((chunks, 3)),
+            sem((chunks, 4)),
             sem((3,)),
             sem((3,)),
             sem,
@@ -423,8 +475,8 @@
         cost_estimate=pl.CostEstimate(flops=flops, bytes_accessed=1 << 24, transcendentals=0),
     )(
         grad_out,
-        routes,
-        route_weight,
+        routes.T,
+        route_weight.T,
         hidden.reshape(slots, hidden_width),
         down_weight.reshape(quarter, width),
     )

time: 285 us -> 248 us (0.87)
  Pallas kernels: 274 us -> 240 us
  local copies, waits for them, and re-layouts: 4.57 us -> 1.72 us
    pallas_call x1, Pallas kernels: 274 us -> 240 us  [per_device(): pl.pallas_call(functools.partial(kernel, n, cap, tokens, chunk, chunks, q...]
where the time goes in v2:
time: 248 us
  Pallas kernels  240 us (97%)
  other arithmetic  4.98 us (2%)
    pallas_call x1, Pallas kernels, per_device(): pl.pallas_call(functools.partial(kernel, n, cap, tokens, chunk, chunks, q...  240 us
    reshape x1, other arithmetic, per_device(): down_grad.reshape(1, quarter, width)  4.98 us

profile of v2, /device:TPU:1, one launch (start us, length us, event | category | flops | bytes accessed | tf_op | source)
XLA Modules:
  0.0 247.7 jit_solution(14421178884158637627)
XLA Ops:
  0.6 240.4 %shard_map.76 = (f32[256,3584]{1,0:T(8,128)}, bf16[256,3584]{1,0:T(8,128)(2,1)}, bf16[640,1024]{1,0:T(8,128)(2,1)}, f32[160,2]{1,0:T(8,128)}) custom-call(bf16[160,3584]{1,0:T(8,128)(2,1)} %grad_ref.1, s32[2,160]{1,0:T(2,128)} %bitcast.18, bf16[2,160]{1,0:T(2,128)(2,1)} %bitcast.19, bf16[640,1024]{1,0:T(8,128)(2,1)} %bitcast.17, bf16[256,3584]{1,0:T(8,128)(2,1)} %bitcast.16), custom_call_target="tpu_custom_call" | custom-call | flops 18320719872 | bytes 16777216 | tf_op jit(solution)/shard_map/pallas_call | solution.py:416
  241.0 0.0 copy-start.1
  241.0 0.0 copy-start
  241.0 5.0 %add_bitcast_fusion = f32[1,256,3584]{2,1,0:T(8,128)} fusion(f32[256,3584]{1,0:T(8,128)} %get-tuple-element.7, bf16[256,3584]{1,0:T(8,128)(2,1)} %get-tuple-element.8), kind=kLoop, calls=%fused_computation | loop fusion | flops 1835008 | bytes 9175040 | tf_op jit(solution)/shard_map/reshape | solution.py:486
  246.0 0.0 copy-done.1
  246.0 0.7 copy.8
  246.7 0.0 copy-done
  246.7 1.1 copy.10
Async XLA Ops:
  241.0 5.0 %copy-start.1 = (f32[160,2]{1,0:T(8,128)S(1)}, f32[160,2]{1,0:T(8,128)}, u32[]{:S(2)}) copy-start(f32[160,2]{1,0:T(8,128)} %get-tuple-element.13) | copy-start | bytes 3844
  241.0 5.7 %copy-start = (bf16[640,1024]{1,0:T(8,128)(2,1)S(1)}, bf16[640,1024]{1,0:T(8,128)(2,1)}, u32[]{:S(2)}) copy-start(bf16[640,1024]{1,0:T(8,128)(2,1)} %get-tuple-element.9) | copy-start | bytes 3932164

commit v3 on v2

--- a/solution.py
+++ b/solution.py
@@ -169,9 +169,6 @@
     hid_copy.start()
     send_tokens(2)
 
-    to = iota((slots, n * WIDE), 0)
-    to = (to % n) * WIDE + (to % (2 * n)) // n * cap + to // (2 * n)
-    order_back[...] = (iota((slots, n * WIDE), 1) == to).astype(F32).astype(BF16)
     hand_on(0)
 
     for copy in meta_copies:
@@ -292,8 +289,7 @@
         lax.fori_loop(0, rows // tile, turn, 0)
 
     def down(k):
-        if k < chunks - 1:
-            row_wait(k).wait_recv()
+        row_wait(k).wait_recv()
         if k == 0:
             weigh_hidden()
         into = buffers(k)[1]
@@ -321,21 +317,39 @@
 
         lax.fori_loop(0, 6, step, 0)
 
+    def order_slots():
+        to = iota((slots, n * WIDE), 0)
+        to = (to % n) * WIDE + (to % (2 * n)) // n * cap + to // (2 * n)
+        order_back[...] = (iota((slots, n * WIDE), 1) == to).astype(F32).astype(BF16)
+
+    meet = 1
+    lag = 3
     for k in range(chunks):
-        if k + 1 < chunks:
+        if 1 <= k < chunks - 1:
             hand_on(k + 1)
         gather(k)
+        if k == 0:
+            hand_on(1)
         if k + 3 < chunks:
             send_tokens(k + 3)
-        w_loads[k].wait()
-        w_copies[k].start()
-        if k == 0:
+        for m in ((0, 1, 2) if k == 0 else (k + 2,)):
+            if m < chunks:
+                w_loads[m].wait()
+                w_copies[m].start()
+        if k == 1:
+            order_slots()
+        if k == meet:
             order_hidden()
-        if k >= 1:
+            for m in range(k):
+                down(m)
+        if k > meet:
             down(k - 1)
-            project(k - 1)
-
-    row_wait(chunks - 1).wait_recv()
+        if k > lag:
+            project(k - 1 - lag)
+
+    for k in range(chunks - 1 - lag, chunks - 1):
+        project(k)
+    down(chunks - 1)
     project(chunks - 1)
     hg_columns = pl.ds(pl.multiple_of(hh * half, half), half)
     hg_copy = remote(hg_send, hg_ref.at[:, hg_columns], hg_ssem, hg_rsem, (da, e))
@@ -347,8 +361,6 @@
         got = (got * gate).reshape(n * WIDE, half).astype(BF16)
         return jnp.dot(order_back[...], got, preferred_element_type=F32).astype(BF16)
 
-    hg_send[...] = weigh(1)
-    hg_copy.start()
     sums = jnp.sum(hid_rows[...].astype(F32) * q[...], axis=1, keepdims=True)
     spread = jnp.where(
         iota((rows, LANES), 1) == iota((rows, LANES), 0) % WIDE, sums, 0.0
@@ -357,7 +369,8 @@
     part_out[...] = spread[:, 1]
     part_copy = remote(part_out, part_in, part_ssem, part_rsem, (da, e))
     part_copy.start()
-    down(chunks - 1)
+    hg_send[...] = weigh(1)
+    hg_copy.start()
     hg_own[...] = weigh(0)
     hg_store.start()
     part_copy.wait_recv()

time: 248 us -> 223 us (0.90)
  Pallas kernels: 240 us -> 215 us
    pallas_call x1, Pallas kernels: 240 us -> 215 us  [per_device(): pl.pallas_call(functools.partial(kernel, n, cap, tokens, chunk, chunks, q...]
where the time goes in v3:
time: 223 us
  Pallas kernels  215 us (96%)
  other arithmetic  4.98 us (2%)
    pallas_call x1, Pallas kernels, per_device(): pl.pallas_call(functools.partial(kernel, n, cap, tokens, chunk, chunks, q...  215 us
    reshape x1, other arithmetic, per_device(): down_grad.reshape(1, quarter, width)  4.98 us

profile of v3, /device:TPU:1, one launch (start us, length us, event | category | flops | bytes accessed | tf_op | source)
XLA Modules:
  0.0 222.8 jit_solution(7110200724449136149)
XLA Ops:
  0.6 215.4 %shard_map.76 = (f32[256,3584]{1,0:T(8,128)}, bf16[256,3584]{1,0:T(8,128)(2,1)}, bf16[640,1024]{1,0:T(8,128)(2,1)}, f32[160,2]{1,0:T(8,128)}) custom-call(bf16[160,3584]{1,0:T(8,128)(2,1)} %grad_ref.1, s32[2,160]{1,0:T(2,128)} %bitcast.18, bf16[2,160]{1,0:T(2,128)(2,1)} %bitcast.19, bf16[640,1024]{1,0:T(8,128)(2,1)} %bitcast.17, bf16[256,3584]{1,0:T(8,128)(2,1)} %bitcast.16), custom_call_target="tpu_custom_call" | custom-call | flops 18320719872 | bytes 16777216 | tf_op jit(solution)/shard_map/pallas_call | solution.py:429
  216.1 0.0 copy-start.1
  216.1 0.0 copy-start
  216.1 5.0 %add_bitcast_fusion = f32[1,256,3584]{2,1,0:T(8,128)} fusion(f32[256,3584]{1,0:T(8,128)} %get-tuple-element.7, bf16[256,3584]{1,0:T(8,128)(2,1)} %get-tuple-element.8), kind=kLoop, calls=%fused_computation | loop fusion | flops 1835008 | bytes 9175040 | tf_op jit(solution)/shard_map/reshape | solution.py:499
  221.1 0.0 copy-done.1
  221.1 0.7 copy.8
  221.7 0.0 copy-done
  221.7 1.1 copy.10
Async XLA Ops:
  216.1 5.0 %copy-start.1 = (f32[160,2]{1,0:T(8,128)S(1)}, f32[160,2]{1,0:T(8,128)}, u32[]{:S(2)}) copy-start(f32[160,2]{1,0:T(8,128)} %get-tuple-element.13) | copy-start | bytes 3844
  216.1 5.7 %copy-start = (bf16[640,1024]{1,0:T(8,128)(2,1)S(1)}, bf16[640,1024]{1,0:T(8,128)(2,1)}, u32[]{:S(2)}) copy-start(bf16[640,1024]{1,0:T(8,128)(2,1)} %get-tuple-element.9) | copy-start | bytes 3932164

commit v4 on v3

--- a/solution.py
+++ b/solution.py
@@ -22,7 +22,7 @@
     n, cap, tokens, chunk, chunks, quarter,
     grad_ref, routes_ref, gate_ref, hidden_ref, weight_ref,
     own_ref, other_ref, hg_ref, prob_ref,
-    tok, meta, place0, place1, onehot, order_back, send0, recv0, send, recv,
+    tok, meta, place0, place1, gates0, gates1, onehot, order_back, send0, recv0, send, recv,
     wbuf, hid_all, hid_part, hid_rows, hid_t, q,
     dg_own, dg_send, hg_own, hg_send, part_out, part_in, back_out, back_in,
     load_sem, tok_ssem, tok_rsem, meta_ssem, meta_rsem, hid_ssem, hid_rsem,
@@ -123,42 +123,18 @@
         near.wait_send()
         pl.when(inner)(both.wait_send)
 
-    send_tokens(0)
-
-    lane = iota((tokens, LANES), 1)
-    lane_f = lane.astype(F32)
-
-    def column(array, k):
-        pick = (iota((2, LANES), 0) == k).astype(F32).astype(BF16)
-        return lax.dot_general(
-            array, pick, (((0,), (0,)), ((), ())), preferred_element_type=F32
-        )
-
-    experts = routes_ref[...].astype(F32).astype(BF16)
-    name0, name1 = column(experts, 0), column(experts, 1)
-    member0 = (lane_f == name0).astype(F32)
-    member1 = (lane_f == name1).astype(F32)
-    before = (iota((tokens, tokens), 1) < iota((tokens, tokens), 0)).astype(F32).astype(BF16)
-    earlier = jnp.dot(before, (member0 + member1).astype(BF16), preferred_element_type=F32)
-    slot0 = jnp.sum(earlier * member0, axis=1, keepdims=True)
-    slot1 = jnp.sum(earlier * member1, axis=1, keepdims=True)
-    gates = gate_ref[...]
-    info = jnp.where(lane == 0, name0, 0.0)
-    info = jnp.where(lane == 1, name1, info)
-    info = jnp.where(lane == 2, column(gates, 0), info)
-    info = jnp.where(lane == 3, column(gates, 1), info)
-    info = jnp.where(lane == 4, slot0, info)
-    info = jnp.where(lane == 5, slot1, info)
-    meta[pl.ds(own_block, tokens), :] = info.astype(BF16)
-    meta_here = meta.at[pl.ds(own_block, tokens)]
-    meta_there = meta.at[pl.ds(pl.multiple_of((2 + zl) * tokens, tokens), tokens)]
+    meta[zl] = jnp.zeros((16, 256), BF16)
+    meta[zl, 0:2, 0:tokens] = routes_ref[...].astype(F32).astype(BF16)
+    meta[zl, 2:4, 0:tokens] = gate_ref[...]
     meta_copies = [
-        remote(meta_here, meta_here, meta_ssem.at[0], meta_rsem.at[0], (d, across)),
-        remote(meta_here, meta_there, meta_ssem.at[1], meta_rsem.at[1], (da, e)),
-        remote(meta_here, meta_there, meta_ssem.at[2], meta_rsem.at[2], (da, across)),
+        remote(meta.at[zl], meta.at[zl], meta_ssem.at[0], meta_rsem.at[0], (d, across)),
+        remote(meta.at[zl], meta.at[2 + zl], meta_ssem.at[1], meta_rsem.at[1], (da, e)),
+        remote(meta.at[zl], meta.at[2 + zl], meta_ssem.at[2], meta_rsem.at[2], (da, across)),
     ]
     for copy in meta_copies:
         copy.start()
+    send_tokens(0)
+
     send_tokens(1)
 
     hid_load.wait()
@@ -173,15 +149,34 @@
 
     for copy in meta_copies:
         copy.wait_recv()
+    lane_f = iota((tokens, LANES), 1).astype(F32)
+    before = (iota((tokens, tokens), 1) < iota((tokens, tokens), 0)).astype(F32).astype(BF16)
+
+    def column(block, k):
+        pick = (iota((2, LANES), 0) == k % 2).astype(F32).astype(BF16)
+        row = meta[block, k // 2 * 2 : k // 2 * 2 + 2, 0:tokens]
+        return lax.dot_general(
+            row, pick, (((0,), (0,)), ((), ())), preferred_element_type=F32
+        )
+
+    def slots_of(block):
+        names = column(block, 0), column(block, 1)
+        members = [(lane_f == name).astype(F32) for name in names]
+        earlier = jnp.dot(
+            before, (members[0] + members[1]).astype(BF16), preferred_element_type=F32
+        )
+        places = [jnp.sum(earlier * member, axis=1, keepdims=True) for member in members]
+        return names, members, places
+
     plane = (zl * rows).astype(F32)
     for block in range(4):
         part = pl.ds(block * tokens, tokens)
         offset = float((block // 2) * WIDE + (block % 2) * cap)
-        seen = meta[part, :].astype(F32)
-        at = seen[:, 0:1] * span + seen[:, 4:5] - plane + offset
-        place0[part, :] = jnp.broadcast_to(at, (tokens, LANES))
-        at = seen[:, 1:2] * span + seen[:, 5:6] - plane + offset
-        place1[part, :] = jnp.broadcast_to(at, (tokens, LANES))
+        names, _, places = slots_of(block)
+        place0[part, :] = names[0] * span + (places[0] - plane + offset)
+        place1[part, :] = names[1] * span + (places[1] - plane + offset)
+        gates0[part, :] = column(block, 2).astype(BF16)
+        gates1[part, :] = column(block, 3).astype(BF16)
 
     tile = min(LANES, rows)
 
@@ -191,10 +186,8 @@
         first = (place0[...] == row).astype(F32).astype(BF16).T
         second = (place1[...] == row).astype(F32).astype(BF16).T
         onehot[part, :] = (first + second)[:tile]
-        gate0 = jnp.broadcast_to(meta[:, 2:3], (4 * tokens, LANES))
-        gate1 = jnp.broadcast_to(meta[:, 3:4], (4 * tokens, LANES))
-        gate = jnp.dot(first, gate0, preferred_element_type=F32)
-        gate = gate + jnp.dot(second, gate1, preferred_element_type=F32)
+        gate = jnp.dot(first, gates0[...], preferred_element_type=F32)
+        gate = gate + jnp.dot(second, gates1[...], preferred_element_type=F32)
         send0[part, pl.ds(chunk, LANES)] = gate[:tile].astype(BF16)
         return carry
 
@@ -389,7 +382,13 @@
     many = pl.ds(0, 2 * n - 1)
     remote(back_in.at[many], back_in.at[many], back_ssem, back_rsem, (db, e)).wait()
     table = back_in[...][:, 0, :]
-    for k, (member, slot) in enumerate(((member0, slot0), (member1, slot1))):
+    own_rows_in = pl.ds(own_block, tokens)
+    base = plane - (zl * cap).astype(F32)
+    for k, place in enumerate((place0, place1)):
+        at = place[own_rows_in, :] + base
+        name = jnp.floor((at + 0.5) / span)
+        member = (lane_f == name).astype(F32)
+        slot = (at - name * span)[:, 0:1]
         found = jnp.dot(
             member[:, : 2 * n], table, preferred_element_type=F32, precision=lax.Precision.HIGHEST
         )
@@ -438,9 +437,11 @@
         out_specs=(anywhere, anywhere, anywhere, vmem),
         scratch_shapes=[
             pltpu.VMEM((chunks, 4 * tokens, chunk), BF16),
-            pltpu.VMEM((4 * tokens, LANES), BF16),
+            pltpu.VMEM((4, 16, 256), BF16),
             pltpu.VMEM((4 * tokens, LANES), F32),
             pltpu.VMEM((4 * tokens, LANES), F32),
+            pltpu.VMEM((4 * tokens, LANES), BF16),
+            pltpu.VMEM((4 * tokens, LANES), BF16),
             pltpu.VMEM((rows, 4 * tokens), BF16),
             pltpu.VMEM((slots, n * WIDE), BF16),
             pltpu.VMEM((rows, chunk + LANES), BF16),

time: 223 us -> 221 us (level)
  no operation moved by 1% of the time
where the time goes in v4:
time: 221 us
  Pallas kernels  214 us (97%)
  other arithmetic  4.98 us (2%)
    pallas_call x1, Pallas kernels, per_device(): pl.pallas_call(functools.partial(kernel, n, cap, tokens, chunk, chunks, q...  214 us
    reshape x1, other arithmetic, per_device(): down_grad.reshape(1, quarter, width)  4.98 us

profile of v4, /device:TPU:1, one launch (start us, length us, event | category | flops | bytes accessed | tf_op | source)
XLA Modules:
  0.0 220.9 jit_solution(13255717767109615367)
XLA Ops:
  0.6 213.5 %shard_map.76 = (f32[256,3584]{1,0:T(8,128)}, bf16[256,3584]{1,0:T(8,128)(2,1)}, bf16[640,1024]{1,0:T(8,128)(2,1)}, f32[160,2]{1,0:T(8,128)}) custom-call(bf16[160,3584]{1,0:T(8,128)(2,1)} %grad_ref.1, s32[2,160]{1,0:T(2,128)} %bitcast.18, bf16[2,160]{1,0:T(2,128)(2,1)} %bitcast.19, bf16[640,1024]{1,0:T(8,128)(2,1)} %bitcast.17, bf16[256,3584]{1,0:T(8,128)(2,1)} %bitcast.16), custom_call_target="tpu_custom_call" | custom-call | flops 18320719872 | bytes 16777216 | tf_op jit(solution)/shard_map/pallas_call | solution.py:428
  214.2 0.0 copy-start.1
  214.2 0.0 copy-start
  214.2 5.0 %add_bitcast_fusion = f32[1,256,3584]{2,1,0:T(8,128)} fusion(f32[256,3584]{1,0:T(8,128)} %get-tuple-element.7, bf16[256,3584]{1,0:T(8,128)(2,1)} %get-tuple-element.8), kind=kLoop, calls=%fused_computation | loop fusion | flops 1835008 | bytes 9175040 | tf_op jit(solution)/shard_map/reshape | solution.py:500
  219.2 0.0 copy-done.1
  219.2 0.7 copy.8
  219.8 0.0 copy-done
  219.8 1.1 copy.10
Async XLA Ops:
  214.2 5.0 %copy-start.1 = (f32[160,2]{1,0:T(8,128)S(1)}, f32[160,2]{1,0:T(8,128)}, u32[]{:S(2)}) copy-start(f32[160,2]{1,0:T(8,128)} %get-tuple-element.13) | copy-start | bytes 3844
  214.2 5.7 %copy-start = (bf16[640,1024]{1,0:T(8,128)(2,1)S(1)}, bf16[640,1024]{1,0:T(8,128)(2,1)}, u32[]{:S(2)}) copy-start(bf16[640,1024]{1,0:T(8,128)(2,1)} %get-tuple-element.9) | copy-start | bytes 3932164

commit v5 on v4

--- a/solution.py
+++ b/solution.py
@@ -142,8 +142,8 @@
         hid_all.at[:, pl.ds(pl.multiple_of((1 - hh) * half, half), half)],
         hid_part, hid_ssem, hid_rsem, (da, e),
     )
+    send_tokens(2)
     hid_copy.start()
-    send_tokens(2)
 
     hand_on(0)
 

time: 221 us -> 222 us (level)
  no operation moved by 1% of the time
where the time goes in v5:
time: 222 us
  Pallas kernels  214 us (96%)
  other arithmetic  4.98 us (2%)
    pallas_call x1, Pallas kernels, per_device(): pl.pallas_call(functools.partial(kernel, n, cap, tokens, chunk, chunks, q...  214 us
    reshape x1, other arithmetic, per_device(): down_grad.reshape(1, quarter, width)  4.98 us

profile of v5, /device:TPU:1, one launch (start us, length us, event | category | flops | bytes accessed | tf_op | source)
XLA Modules:
  0.0 221.8 jit_solution(1846829129322074962)
XLA Ops:
  0.6 214.4 %shard_map.76 = (f32[256,3584]{1,0:T(8,128)}, bf16[256,3584]{1,0:T(8,128)(2,1)}, bf16[640,1024]{1,0:T(8,128)(2,1)}, f32[160,2]{1,0:T(8,128)}) custom-call(bf16[160,3584]{1,0:T(8,128)(2,1)} %grad_ref.1, s32[2,160]{1,0:T(2,128)} %bitcast.18, bf16[2,160]{1,0:T(2,128)(2,1)} %bitcast.19, bf16[640,1024]{1,0:T(8,128)(2,1)} %bitcast.17, bf16[256,3584]{1,0:T(8,128)(2,1)} %bitcast.16), custom_call_target="tpu_custom_call" | custom-call | flops 18320719872 | bytes 16777216 | tf_op jit(solution)/shard_map/pallas_call | solution.py:428
  215.0 0.0 copy-start.1
  215.0 0.0 copy-start
  215.1 5.0 %add_bitcast_fusion = f32[1,256,3584]{2,1,0:T(8,128)} fusion(f32[256,3584]{1,0:T(8,128)} %get-tuple-element.7, bf16[256,3584]{1,0:T(8,128)(2,1)} %get-tuple-element.8), kind=kLoop, calls=%fused_computation | loop fusion | flops 1835008 | bytes 9175040 | tf_op jit(solution)/shard_map/reshape | solution.py:500
  220.0 0.0 copy-done.1
  220.0 0.7 copy.8
  220.7 0.0 copy-done
  220.7 1.1 copy.10
Async XLA Ops:
  215.0 5.0 %copy-start.1 = (f32[160,2]{1,0:T(8,128)S(1)}, f32[160,2]{1,0:T(8,128)}, u32[]{:S(2)}) copy-start(f32[160,2]{1,0:T(8,128)} %get-tuple-element.13) | copy-start | bytes 3844
  215.0 5.7 %copy-start = (bf16[640,1024]{1,0:T(8,128)(2,1)S(1)}, bf16[640,1024]{1,0:T(8,128)(2,1)}, u32[]{:S(2)}) copy-start(bf16[640,1024]{1,0:T(8,128)(2,1)} %get-tuple-element.9) | copy-start | bytes 3932164
